TPU v7x, 256 devices: a whole 4x4x8 slice. The times are simulated.
256 devices in a mesh: seq: 16 (over y, z_hi), tp: 16 (over z_lo, x, core).
Axes of the slice: x: 4, y: 4, z: 8 (z_hi: 4, z_lo: 2; z = z_hi * 2 + z_lo), core: 2. Of those that a mesh axis runs over, the one named last changes fastest.
Arguments:
- spatial_input_rows: bfloat16 [2, 16, 128, 3072], P(None, 'seq', None, 'tp'), may hold values from -6 to 6
- x_temporal: bfloat16 [2, 16, 128, 3072], P(None, 'seq', None, 'tp'), may hold values from -6 to 6
- cotangent: bfloat16 [2, 16, 128, 3072], P(None, 'seq', None, 'tp'), may hold values from -6 to 6
- spatial_query_key_value: bfloat16 [3072, 3, 2048], P(None, None, 'tp'), may hold values from -0.109375 to 0.109375
- spatial_output_weight: bfloat16 [2048, 3072], P('tp'), may hold values from -0.125 to 0.125
- temporal_query_key_value: bfloat16 [3072, 3, 2048], P(None, None, 'tp'), may hold values from -0.109375 to 0.109375
- temporal_output_weight: bfloat16 [2048, 3072], P('tp'), may hold values from -0.125 to 0.125
- up_weight: bfloat16 [3072, 6144], P(None, 'tp'), may hold values from -0.109375 to 0.109375
- down_weight: bfloat16 [6144, 3072], P('tp'), may hold values from -0.078125 to 0.078125
Outputs:
- spatial_input_gradient: bfloat16 [2, 16, 128, 3072], P(None, 'seq', None, 'tp')
- grad_qkv_spatial: bfloat16 [3072, 3, 2048], P('seq', None, 'tp')
- grad_out_spatial: bfloat16 [2048, 3072], P('tp', 'seq')
- grad_qkv_temporal: bfloat16 [3072, 3, 2048], P('seq', None, 'tp')
- grad_out_temporal: bfloat16 [2048, 3072], P('tp', 'seq')
- grad_up: bfloat16 [3072, 6144], P('seq', 'tp')
- grad_down: bfloat16 [6144, 3072], P('tp', 'seq')
All inputs are finite; a program needn't handle non-finite values.
Results may differ from a plain program's by a relative error of at most 0.04.
Values may be sent and summed in bfloat16 or wider, within the bound.
No kernel may reach another device: no remote copies, remote signals or barrier semaphores. Data moves between devices by JAX's collectives and lax.ppermute only.
A program may use at most 128 MiB of HBM per device.

v0:
```python
import math

import jax
import jax.numpy as jnp
from jax import lax
from jax.sharding import PartitionSpec as P

HDIM = 128
FRAMES = 16
PATCHES = 128
SEQS = 2


EPS = 1e-06
ROOT = 0.7978845608028654
CUBIC = 0.044715
SPATIAL_FORMS = ("bfqnh,bfknh->bfnqk", "bfnqk,bfknh->bfqnh", "bfnqk,bfqnh->bfknh")
TEMPORAL_FORMS = ("bqpnh,bkpnh->bpnqk", "bpnqk,bkpnh->bqpnh", "bpnqk,bqpnh->bkpnh")


def gelu_value(pre_act):
    inner_product = jnp.tanh(ROOT * (pre_act + CUBIC * pre_act * pre_act * pre_act))
    return 0.5 * pre_act * (1.0 + inner_product)


def gelu_slope(pre_act):
    inner_product = jnp.tanh(ROOT * (pre_act + CUBIC * pre_act * pre_act * pre_act))
    return 0.5 * (1.0 + inner_product) + 0.5 * pre_act * (
        1.0 - inner_product * inner_product
    ) * ROOT * (1.0 + 3.0 * CUBIC * pre_act * pre_act)


def apply_norm(values):
    wide = values.astype(jnp.float32)
    inverse_norm = lax.rsqrt(jnp.mean(wide * wide, axis=-1, keepdims=True) + EPS)
    return (inverse_norm, wide * inverse_norm)


def gather_features(values):
    return lax.all_gather(values, "tp", axis=3, tiled=True)


def head_whole(portion_value):
    return lax.psum(portion_value.astype(jnp.bfloat16), "tp").astype(jnp.float32)


def norm_reduction(portion_value, gradient_complete, gradient_portion, inverse_norm, centered_rows):
    width = gradient_portion.shape[3]
    running_total = head_whole(portion_value)
    inner_product = jnp.mean(running_total * centered_rows, axis=-1, keepdims=True)
    complete_rows = (
        gradient_complete.astype(jnp.float32)
        + inverse_norm * (running_total - centered_rows * inner_product)
    ).astype(jnp.bfloat16)
    own_part = lax.dynamic_slice_in_dim(complete_rows, lax.axis_index("tp") * width, width, 3)
    return (own_part, complete_rows)


def column_grads(left, right, scale_factor):
    term = scale_factor * jnp.einsum(
        "bfpa,bfpd->ad", left, right, preferred_element_type=jnp.float32
    )
    return lax.psum_scatter(term.astype(jnp.bfloat16), "seq", scatter_dimension=1, tiled=True)


def row_grads(left, right, scale_factor):
    return lax.psum_scatter(
        (
            scale_factor
            * jnp.einsum("bfpd,bfpc->dc", left, right, preferred_element_type=jnp.float32)
        ).astype(jnp.bfloat16),
        "seq",
        scatter_dimension=0,
        tiled=True,
    )


def qkv_grads(normed_rows, d_qkv, scale_factor):
    flat = d_qkv.reshape(d_qkv.shape[:3] + (3 * d_qkv.shape[4],))
    return row_grads(normed_rows, flat, scale_factor).reshape(-1, 3, d_qkv.shape[4])


def attend(normed_rows, query_key_value_weight, forms):
    heads = query_key_value_weight.shape[2] // HDIM
    joined = jnp.einsum(
        "bfpd,dkh->bfpkh", normed_rows, query_key_value_weight, preferred_element_type=jnp.float32
    ).astype(jnp.bfloat16)
    joined = joined.reshape(joined.shape[:4] + (heads, HDIM))
    query = joined[:, :, :, 0]
    keyset = joined[:, :, :, 1]
    values = joined[:, :, :, 2]
    scores = jnp.einsum(forms[0], query, keyset, preferred_element_type=jnp.float32) / math.sqrt(
        HDIM
    )
    row_max = jnp.max(scores, axis=-1, keepdims=True)
    raised = jnp.exp(scores - row_max)
    attn_prob = raised / jnp.sum(raised, axis=-1, keepdims=True)
    attn_weights = attn_prob.astype(jnp.bfloat16)
    context = jnp.einsum(forms[1], attn_weights, values, preferred_element_type=jnp.float32).astype(
        jnp.bfloat16
    )
    context = context.reshape(context.shape[:3] + (heads * HDIM,))
    return (query, keyset, values, attn_prob, attn_weights, context)


def attend_back(portion_count, gradient_complete, output_matrix, forms):
    query, keyset, values, attn_prob, attn_weights, context = portion_count
    d_context = jnp.einsum(
        "bfpd,hd->bfph", gradient_complete, output_matrix, preferred_element_type=jnp.float32
    ).astype(jnp.bfloat16)
    d_heads = d_context.reshape(query.shape)
    d_values = jnp.einsum(
        forms[2], attn_weights, d_heads, preferred_element_type=jnp.float32
    ).astype(jnp.bfloat16)
    d_probs = jnp.einsum(forms[0], d_heads, values, preferred_element_type=jnp.float32)
    d_scores = (
        attn_prob
        * (d_probs - jnp.sum(attn_prob * d_probs, axis=-1, keepdims=True))
        / math.sqrt(HDIM)
    ).astype(jnp.bfloat16)
    d_query = jnp.einsum(forms[1], d_scores, keyset, preferred_element_type=jnp.float32).astype(
        jnp.bfloat16
    )
    d_keys = jnp.einsum(forms[2], d_scores, query, preferred_element_type=jnp.float32).astype(
        jnp.bfloat16
    )
    stacked = jnp.stack((d_query, d_keys, d_values), axis=3)
    return stacked.reshape(query.shape[:3] + (3, output_matrix.shape[0]))


def per_device(
    spatial_input_rows,
    x_temporal,
    cotangent,
    spatial_query_key_value,
    spatial_output_weight,
    temporal_query_key_value,
    temporal_output_weight,
    up_weight,
    down_weight,
):
    scale_factor = (SEQS * FRAMES * PATCHES) ** (-0.5)
    temporal_part, upper_portion = (
        lax.all_to_all(x_temporal, "seq", split_axis=2, concat_axis=1, tiled=True),
        lax.all_to_all(cotangent, "seq", split_axis=2, concat_axis=1, tiled=True),
    )
    temporal_complete, upper_complete = (
        lax.all_gather(temporal_part, "tp", axis=3, tiled=True),
        lax.all_gather(upper_portion, "tp", axis=3, tiled=True),
    )
    temporal_inverse_norm, temporal_centered_rows = apply_norm(temporal_complete)
    temporal_normed_rows = temporal_centered_rows.astype(jnp.bfloat16)
    temporal_portions = attend(temporal_normed_rows, temporal_query_key_value, TEMPORAL_FORMS)
    context_t = temporal_portions[5]
    attn_part = jnp.einsum(
        "bfph,hd->bfpd", context_t, temporal_output_weight, preferred_element_type=jnp.float32
    )
    middle_state = (temporal_complete.astype(jnp.float32) + head_whole(attn_part)).astype(
        jnp.bfloat16
    )
    mlp_inverse_norm, mlp_centered_rows = apply_norm(middle_state)
    mlp_normed_rows = mlp_centered_rows.astype(jnp.bfloat16)
    pre_act = jnp.einsum(
        "bfpd,dc->bfpc", mlp_normed_rows, up_weight, preferred_element_type=jnp.float32
    )
    hidden = gelu_value(pre_act).astype(jnp.bfloat16)
    d_act = jnp.einsum(
        "bfpd,cd->bfpc", upper_complete, down_weight, preferred_element_type=jnp.float32
    )
    d_pre = (d_act * gelu_slope(pre_act)).astype(jnp.bfloat16)
    grad_down = column_grads(hidden, upper_complete, scale_factor)
    grad_up = row_grads(mlp_normed_rows, d_pre, scale_factor)
    mlp_norm_gradient = jnp.einsum(
        "bfpc,dc->bfpd", d_pre, up_weight, preferred_element_type=jnp.float32
    )
    middle_portion, middle_complete = norm_reduction(
        mlp_norm_gradient, upper_complete, upper_portion, mlp_inverse_norm, mlp_centered_rows
    )
    d_qkv_t = attend_back(
        temporal_portions, middle_complete, temporal_output_weight, TEMPORAL_FORMS
    )
    temporal_output_gradient = column_grads(context_t, middle_complete, scale_factor)
    temporal_projection_gradient = qkv_grads(temporal_normed_rows, d_qkv_t, scale_factor)
    temporal_norm_gradient = jnp.einsum(
        "bfpkh,dkh->bfpd", d_qkv_t, temporal_query_key_value, preferred_element_type=jnp.float32
    )
    temporal_grad_rows, discarded_value = norm_reduction(
        temporal_norm_gradient,
        middle_complete,
        middle_portion,
        temporal_inverse_norm,
        temporal_centered_rows,
    )
    frame_grad_rows = lax.all_to_all(
        temporal_grad_rows, "seq", split_axis=1, concat_axis=2, tiled=True
    )
    spatial_complete = gather_features(spatial_input_rows)
    frame_full_rows = gather_features(frame_grad_rows)
    spatial_inverse_norm, spatial_centered_rows = apply_norm(spatial_complete)
    spatial_normed_rows = spatial_centered_rows.astype(jnp.bfloat16)
    spatial_portions = attend(spatial_normed_rows, spatial_query_key_value, SPATIAL_FORMS)
    d_qkv_s = attend_back(spatial_portions, frame_full_rows, spatial_output_weight, SPATIAL_FORMS)
    spatial_output_gradient = column_grads(spatial_portions[5], frame_full_rows, scale_factor)
    spatial_projection_gradient = qkv_grads(spatial_normed_rows, d_qkv_s, scale_factor)
    spatial_norm_gradient = jnp.einsum(
        "bfpkh,dkh->bfpd", d_qkv_s, spatial_query_key_value, preferred_element_type=jnp.float32
    )
    spatial_input_gradient, remaining_gradient = norm_reduction(
        spatial_norm_gradient,
        frame_full_rows,
        frame_grad_rows,
        spatial_inverse_norm,
        spatial_centered_rows,
    )
    return (
        spatial_input_gradient,
        spatial_projection_gradient,
        spatial_output_gradient,
        temporal_projection_gradient,
        temporal_output_gradient,
        grad_up,
        grad_down,
    )


def solution(mesh):
    placed = (
        P(None, "seq", None, "tp"),
        P(None, "seq", None, "tp"),
        P(None, "seq", None, "tp"),
        P(None, None, "tp"),
        P("tp", None),
        P(None, None, "tp"),
        P("tp", None),
        P(None, "tp"),
        P("tp", None),
    )
    return jax.shard_map(
        per_device,
        mesh=mesh,
        in_specs=placed,
        out_specs=(
            P(None, "seq", None, "tp"),
            P("seq", None, "tp"),
            P("tp", "seq"),
            P("seq", None, "tp"),
            P("tp", "seq"),
            P("seq", "tp"),
            P("tp", "seq"),
        ),
        check_vma=False,
    )
```

profile of v0, /device:TPU:2, one launch (start us, length us, event | category | flops | bytes accessed | tf_op | source)
XLA Modules:
  0.0 1336.7 jit_solution(1512104691107835348)
XLA Ops:
  8.4 21.7 %all_to_all.36 = bf16[2,1,128,192]{3,0,1,2:T(2,128)(2,1)S(1)} all-to-all(bf16[2,1,128,192]{3,0,1,2:T(2,128)(2,1)S(1)} %copy.188), channel_id=1, replica_groups=mesh['seq'=16,'tp'=16] {'seq'}, dimensions={2} | all-to-all | bytes 196608 | tf_op jit(solution)/shard_map/all_to_all | solution.py:144
  32.8 13.3 all_to_all.37
  47.7 53.3 %all-gather.7.cloned.1.call-done = bf16[2,16,8,3072]{1,2,0,3:T(8,128)(2,1)} async-done(((bf16[2,16,8,192]{1,2,0,3:T(8,128)(2,1)}), bf16[2,16,8,3072]{1,2,0,3:T(8,128)(2,1)}) %all-gather.7.cloned.1.call-update) | async-done | bytes 1572880 | tf_op jit(solution)/shard_map/all_gather | solution.py:148
  101.0 13.0 copy.191
  115.9 3.3 fusion.74
  123.0 55.2 %all-gather.5.cloned.1.call-done = bf16[2,16,8,3072]{1,2,0,3:T(8,128)(2,1)} async-done(((bf16[2,16,8,192]{1,2,0,3:T(8,128)(2,1)}), bf16[2,16,8,3072]{1,2,0,3:T(8,128)(2,1)}) %all-gather.5.cloned.1.call-update) | async-done | bytes 1572880 | tf_op jit(solution)/shard_map/all_gather | solution.py:149
  178.1 13.0 copy.187
  191.2 113.1 %all-reduce.5.cloned.1.call-done = bf16[2,16,8,3072]{3,2,1,0:T(8,128)(2,1)} async-done(((bf16[2,16,8,3072]{3,2,1,0:T(8,128)(2,1)}), bf16[2,16,8,3072]{3,2,1,0:T(8,128)(2,1)}) %all-reduce.5.cloned.1.call-update) | async-done | bytes 1572880 | tf_op jit(solution)/shard_map/psum | solution.py:44
  304.2 2.6 fusion.17
  313.1 126.6 %all-reduce.7.cloned.1.call-done = bf16[2,16,8,3072]{3,2,1,0:T(8,128)(2,1)} async-done(((bf16[2,16,8,3072]{3,2,1,0:T(8,128)(2,1)}), bf16[2,16,8,3072]{3,2,1,0:T(8,128)(2,1)}) %all-reduce.7.cloned.1.call-update) | async-done | bytes 1572880 | tf_op jit(solution)/shard_map/psum | solution.py:44
  441.9 2.6 fusion.21
  447.3 3.9 fusion.10
  452.1 126.0 %all-reduce.9.cloned.1.call-done = bf16[2,16,8,3072]{3,2,1,0:T(8,128)(2,1)} async-done(((bf16[2,16,8,3072]{3,2,1,0:T(8,128)(2,1)}), bf16[2,16,8,3072]{3,2,1,0:T(8,128)(2,1)}) %all-reduce.9.cloned.1.call-update) | async-done | bytes 1572880 | tf_op jit(solution)/shard_map/psum | solution.py:44
  581.8 19.8 %all_to_all.38 = bf16[2,16,8,192]{3,2,0,1:T(8,128)(2,1)S(1)} all-to-all(bf16[2,16,8,192]{3,2,0,1:T(8,128)(2,1)S(1)} %copy.205), channel_id=1, replica_groups=mesh['seq'=16,'tp'=16] {'seq'}, dimensions={1} | all-to-all | bytes 196608 | tf_op jit(solution)/shard_map/all_to_all | solution.py:194
  602.5 2.6 fusion.6
  605.1 15.4 %all-gather.11.cloned.1.call-done = bf16[2,1,128,3072]{2,0,1,3:T(2,128)(2,1)} async-done(((bf16[2,1,128,192]{2,0,1,3:T(2,128)(2,1)}), bf16[2,1,128,3072]{2,0,1,3:T(2,128)(2,1)}) %all-gather.11.cloned.1.call-update) | async-done | bytes 1572880 | tf_op jit(solution)/shard_map/all_gather | solution.py:40
  620.5 3.6 copy.210
  624.5 2.8 fusion.67
  627.6 31.1 %all-gather.9.cloned.1.call-done = bf16[2,1,128,3072]{2,0,1,3:T(2,128)(2,1)} async-done(((bf16[2,1,128,192]{2,0,1,3:T(2,128)(2,1)}), bf16[2,1,128,3072]{2,0,1,3:T(2,128)(2,1)}) %all-gather.9.cloned.1.call-update) | async-done | bytes 1572880 | tf_op jit(solution)/shard_map/all_gather | solution.py:40
  658.6 3.6 copy.208
  663.7 3.8 fusion.12
  667.6 3.9 fusion.7
  671.9 3.5 fusion.15
  675.5 4.0 fusion.4
  679.5 4.0 fusion.5
  685.3 66.9 %reduce-scatter.11.cloned.1.call-done = bf16[192,384]{1,0:T(8,128)(2,1)} async-done(((bf16[3072,384]{1,0:T(8,128)(2,1)}), bf16[192,384]{1,0:T(8,128)(2,1)}) %reduce-scatter.11.cloned.1.call-update) | async-done | bytes 147472 | tf_op jit(solution)/shard_map/reduce_scatter | solution.py:67
  753.8 121.2 %all-reduce.11.cloned.1.call-done = bf16[2,1,128,3072]{3,2,0,1:T(8,128)(2,1)} async-done(((bf16[2,1,128,3072]{3,2,0,1:T(8,128)(2,1)}), bf16[2,1,128,3072]{3,2,0,1:T(8,128)(2,1)}) %all-reduce.11.cloned.1.call-update) | async-done | bytes 1572880 | tf_op jit(solution)/shard_map/psum | solution.py:44
  880.1 92.1 %reduce-scatter.7.cloned.1.call-done = bf16[192,384]{1,0:T(8,128)(2,1)} async-done(((bf16[3072,384]{1,0:T(8,128)(2,1)}), bf16[192,384]{1,0:T(8,128)(2,1)}) %reduce-scatter.7.cloned.1.call-update) | async-done | bytes 147472 | tf_op jit(solution)/shard_map/reduce_scatter | solution.py:67
  973.8 86.3 %reduce-scatter.13.cloned.1.call-done = bf16[128,192]{0,1:T(8,128)(2,1)} async-done(((bf16[128,3072]{0,1:T(8,128)(2,1)}), bf16[128,192]{0,1:T(8,128)(2,1)}) %reduce-scatter.13.cloned.1.call-update) | async-done | bytes 49168 | tf_op jit(solution)/shard_map/reduce_scatter | solution.py:63
  1060.2 91.0 %reduce-scatter.17.cloned.1.call-done = bf16[384,192]{0,1:T(8,128)(2,1)} async-done(((bf16[384,3072]{0,1:T(8,128)(2,1)}), bf16[384,192]{0,1:T(8,128)(2,1)}) %reduce-scatter.17.cloned.1.call-update) | async-done | bytes 147472 | tf_op jit(solution)/shard_map/reduce_scatter | solution.py:63
  1151.2 91.1 %reduce-scatter.15.cloned.1.call-done = bf16[192,384]{1,0:T(8,128)(2,1)} async-done(((bf16[3072,384]{1,0:T(8,128)(2,1)}), bf16[192,384]{1,0:T(8,128)(2,1)}) %reduce-scatter.15.cloned.1.call-update) | async-done | bytes 147472 | tf_op jit(solution)/shard_map/reduce_scatter | solution.py:67
  1242.4 87.8 %reduce-scatter.9.cloned.1.call-done = bf16[128,192]{0,1:T(8,128)(2,1)} async-done(((bf16[128,3072]{0,1:T(8,128)(2,1)}), bf16[128,192]{0,1:T(8,128)(2,1)}) %reduce-scatter.9.cloned.1.call-update) | async-done | bytes 49168 | tf_op jit(solution)/shard_map/reduce_scatter | solution.py:63
  (124 shorter events, 40.2 us)
Async XLA Ops:
  7.2 299.7 %copy-start = (bf16[3072,384]{1,0:T(8,128)(2,1)S(1)}, bf16[3072,384]{1,0:T(8,128)(2,1)}, u32[]{:S(2)}) copy-start(bf16[3072,384]{1,0:T(8,128)(2,1)} %param.16) | copy-start | bytes 7077892
  7.2 93.8 %all-gather.7.cloned.1.call-start = ((), (), s32[]{:S(2)}) async-start(), calls=%async_computation.10 | async-start | bytes 13369344 | tf_op jit(solution)/shard_map/all_gather | solution.py:148
  31.7 146.4 %all-gather.5.cloned.1.call-start = ((), (), s32[]{:S(2)}) async-start(), calls=%async_computation.9 | async-start | bytes 13369344 | tf_op jit(solution)/shard_map/all_gather | solution.py:149
  47.7 256.6 %all-reduce.5.cloned.1.call-start = ((), (), s32[]{:S(2)}) async-start(), calls=%async_computation.11 | async-start | bytes 3145728 | tf_op jit(solution)/shard_map/psum | solution.py:44
  115.8 5.3 copy-start.13
  119.2 3.7 copy-start.16
  119.2 3.7 copy-start.18
  122.9 316.8 %all-reduce.7.cloned.1.call-start = ((), (), s32[]{:S(2)}) async-start(), calls=%async_computation.12 | async-start | bytes 3145728 | tf_op jit(solution)/shard_map/psum | solution.py:44
  306.9 2.0 copy-start.9
  306.9 2.7 copy-start.20
  312.8 126.9 %copy-start.7 = (bf16[2,16,8,3072]{3,2,1,0:T(8,128)(2,1)S(1)}, bf16[2,16,8,3072]{3,2,1,0:T(8,128)(2,1)}, u32[]{:S(2)}) copy-start(bf16[2,16,8,3072]{3,2,1,0:T(8,128)(2,1)} %copy-done.6) | copy-start | bytes 4718596
  312.9 265.1 %all-reduce.9.cloned.1.call-start = ((), (), s32[]{:S(2)}) async-start(), calls=%async_computation.13 | async-start | bytes 3145728 | tf_op jit(solution)/shard_map/psum | solution.py:44
  439.7 2.2 copy-start.10
  447.3 4.0 copy-start.15
  451.2 169.3 %all-gather.11.cloned.1.call-start = ((), (), s32[]{:S(2)}) async-start(), calls=%async_computation.15 | async-start | bytes 1671168 | tf_op jit(solution)/shard_map/all_gather | solution.py:40
  452.0 206.7 %all-gather.9.cloned.1.call-start = ((), (), s32[]{:S(2)}) async-start(), calls=%async_computation.14 | async-start | bytes 1671168 | tf_op jit(solution)/shard_map/all_gather | solution.py:40
  452.0 127.9 %copy-start.2 = (bf16[2,16,8,3072]{3,2,1,0:T(8,128)(2,1)S(1)}, bf16[2,16,8,3072]{3,2,1,0:T(8,128)(2,1)}, u32[]{:S(2)}) copy-start(bf16[2,16,8,3072]{3,2,1,0:T(8,128)(2,1)} %copy.191) | copy-start | bytes 4718596
  578.0 1.9 copy-start.12
  602.4 149.8 %reduce-scatter.11.cloned.1.call-start = ((), (), s32[]{:S(2)}) async-start(), calls=%async_computation.19 | async-start | bytes 2506752 | tf_op jit(solution)/shard_map/reduce_scatter | solution.py:67
  605.1 270.0 %all-reduce.11.cloned.1.call-start = ((), (), s32[]{:S(2)}) async-start(), calls=%async_computation.16 | async-start | bytes 3145728 | tf_op jit(solution)/shard_map/psum | solution.py:44
  624.1 3.3 copy-start.4
  627.3 34.9 %copy-start.14 = (bf16[128,3072]{1,0:T(8,128)(2,1)S(1)}, bf16[128,3072]{1,0:T(8,128)(2,1)}, u32[]{:S(2)}) copy-start(bf16[128,3072]{1,0:T(8,128)(2,1)} %param.13) | copy-start | bytes 2359300
  662.2 21.4 %copy-start.3 = (bf16[2,1,128,3072]{3,2,0,1:T(8,128)(2,1)}, bf16[2,1,128,3072]{3,2,0,1:T(8,128)(2,1)S(1)}, u32[]{:S(2)}) copy-start(bf16[2,1,128,3072]{3,2,0,1:T(8,128)(2,1)S(1)} %copy.208) | copy-start | bytes 4718596
  667.5 304.7 %reduce-scatter.7.cloned.1.call-start = ((), (), s32[]{:S(2)}) async-start(), calls=%async_computation.17 | async-start | bytes 2506752 | tf_op jit(solution)/shard_map/reduce_scatter | solution.py:67
  671.6 3.9 copy-start.22
  671.6 388.6 %reduce-scatter.13.cloned.1.call-start = ((), (), s32[]{:S(2)}) async-start(), calls=%async_computation.20 | async-start | bytes 835584 | tf_op jit(solution)/shard_map/reduce_scatter | solution.py:63
  675.4 475.8 %reduce-scatter.17.cloned.1.call-start = ((), (), s32[]{:S(2)}) async-start(), calls=%async_computation.22 | async-start | bytes 2506752 | tf_op jit(solution)/shard_map/reduce_scatter | solution.py:63
  679.5 562.9 %reduce-scatter.15.cloned.1.call-start = ((), (), s32[]{:S(2)}) async-start(), calls=%async_computation.21 | async-start | bytes 2506752 | tf_op jit(solution)/shard_map/reduce_scatter | solution.py:67
  683.6 646.6 %reduce-scatter.9.cloned.1.call-start = ((), (), s32[]{:S(2)}) async-start(), calls=%async_computation.18 | async-start | bytes 835584 | tf_op jit(solution)/shard_map/reduce_scatter | solution.py:63
  875.1 1.9 copy-start.5
  875.1 2.4 copy-start.11
  875.1 455.1 %copy-start.1 = (bf16[3072,384]{1,0:T(8,128)(2,1)S(1)}, bf16[3072,384]{1,0:T(8,128)(2,1)}, u32[]{:S(2)}) copy-start(bf16[3072,384]{1,0:T(8,128)(2,1)} %param.16) | copy-start | bytes 7077892
  (6 other events, 6.7 us)
Sparse Core Ops, SparseCore 0:
  31.8 69.1 all-gather.6
  102.8 75.2 all-gather.4
  180.8 123.4 all-reduce.4
  313.0 126.6 all-reduce.6
  451.3 126.6 all-reduce.8
  580.4 40.0 all-gather.10
  623.1 35.5 all-gather.8
  662.7 89.5 reduce-scatter.10
  755.1 119.9 all-reduce.10
  878.5 93.6 reduce-scatter.6
  976.3 83.8 reduce-scatter.12
  1064.2 86.9 reduce-scatter.16
  1155.4 86.9 reduce-scatter.14
  1246.3 83.8 reduce-scatter.8
where the time goes:
time: 1340 us
  waiting for transfers between devices  1160 us (87%)
  blocking collectives  54.7 us (4%)
  local copies, waits for them, and re-layouts  47.6 us (4%)
  matrix products  44.4 us (3%)
  other arithmetic  17.3 us (1%)
  between operations  14.4 us (1%)
    psum x4, waiting for transfers between devices, head_whole(): lax.psum(portion_value.astype(jnp.bfloat16), 'tp').astype(jnp.float32)  487 us
    reduce_scatter x3, waiting for transfers between devices, column_grads(): lax.psum_scatter(term.astype(jnp.bfloat16), 'seq', scatter_dimension=1, t...  265 us
    reduce_scatter x3, waiting for transfers between devices, row_grads(): lax.psum_scatter((scale_factor * jnp.einsum('bfpd,bfpc->dc', left, right,...  250 us
    all_gather x1, waiting for transfers between devices, per_device(): lax.all_gather(upper_portion, 'tp', axis=3, tiled=True)  55.2 us
    all_gather x1, waiting for transfers between devices, per_device(): lax.all_gather(temporal_part, 'tp', axis=3, tiled=True)  53.3 us
    all_gather x2, waiting for transfers between devices, gather_features(): return lax.all_gather(values, 'tp', axis=3, tiled=True)  46.4 us
  transfers between devices with their start and end apart: 14, of which 14 were waited for; matrix products, arithmetic and copies ran while one was open for 6% of the time, Pallas kernels for 0%

commit v1 on v0

v1 whole, which is shorter than its diff:
```python
import math

import jax
import jax.numpy as jnp
from jax import lax
from jax.sharding import Mesh
from jax.sharding import PartitionSpec as P

D = 3072
HDIM = 128
FRAMES = 16
PATCHES = 128
SEQS = 2
TOKENS = 256
HALF = 128
CHIPS = 8
EPS = 1e-06
ROOT = 0.7978845608028654
CUBIC = 0.044715
SCALE = (SEQS * FRAMES * PATCHES) ** -0.5
SEQ = ("y", "zh")
TP = ("zl", "x", "c")
RING = ("zl", "x")


def gelu_both(pre_act):
    inner = jnp.tanh(ROOT * (pre_act + CUBIC * pre_act * pre_act * pre_act))
    value = 0.5 * pre_act * (1.0 + inner)
    slope = 0.5 * (1.0 + inner) + 0.5 * pre_act * (1.0 - inner * inner) * ROOT * (
        1.0 + 3.0 * CUBIC * pre_act * pre_act
    )
    return value, slope


def dot(left, right, dims):
    return lax.dot_general(left, right, (dims, ((), ())), preferred_element_type=jnp.float32)


def mm(left, right):
    return dot(left, right, ((1,), (0,)))


def mm_nt(left, right):
    return dot(left, right, ((1,), (1,)))


def mm_tn(left, right):
    return dot(left, right, ((0,), (0,)))


def half(values):
    return values.astype(jnp.bfloat16)


def wide(values):
    return values.astype(jnp.float32)


def normalize(values):
    values = wide(values)
    inverse = lax.rsqrt(jnp.mean(values * values, axis=-1, keepdims=True) + EPS)
    return inverse, values * inverse


def normalize_back(residual, inverse, centered, gradient):
    inner = jnp.mean(gradient * centered, axis=-1, keepdims=True)
    return half(wide(residual) + inverse * (gradient - centered * inner))


def swap(values):
    return lax.ppermute(values, "c", [(0, 1), (1, 0)])


def spread(values):
    copies = jnp.broadcast_to(values[None], (CHIPS,) + values.shape)
    return lax.all_to_all(copies, RING, 0, 0, tiled=True)


def features_whole(values):
    count = values.shape[1]
    theirs = swap(values[1])
    first = lax.axis_index("c") == 0
    low = jnp.where(first, values[0], theirs)
    high = jnp.where(first, theirs, values[0])
    joined = jnp.concatenate((low, high), axis=1)
    return jnp.transpose(spread(joined), (1, 0, 2)).reshape(count, D)


def own_first(values):
    core = lax.axis_index("c")
    return jnp.where(core == 0, values, values[::-1])


def both(values):
    return jnp.concatenate((values, swap(values)), axis=0)


def rows_whole(values):
    return both(spread(values).reshape(HALF, D))


def reduce_rows(left, right):
    theirs = swap(half(mm_nt(left[HALF:], right)))
    mine = half(mm_nt(left[:HALF], right) + wide(theirs))
    pieces = lax.all_to_all(mine.reshape(CHIPS, HALF // CHIPS, D), RING, 0, 0, tiled=True)
    return jnp.sum(wide(pieces), axis=0)


def sum_tokens(term):
    pieces = lax.all_to_all(term.reshape(4, D // 4, -1), "y", 0, 0, tiled=True)
    part = half(jnp.sum(wide(pieces), axis=0))
    pieces = lax.all_to_all(part.reshape(4, D // 16, -1), "zh", 0, 0, tiled=True)
    return half(jnp.sum(wide(pieces), axis=0))


def own_rows(values):
    chip = lax.axis_index(RING)
    count = HALF // CHIPS
    return lax.dynamic_slice_in_dim(values[:HALF], chip * count, count, 0)


def attend(normed, weight, span):
    joined = half(mm(normed, weight))
    query, keyset, values = joined[:, :HDIM], joined[:, HDIM : 2 * HDIM], joined[:, 2 * HDIM :]
    scores = mm_nt(query, keyset) / math.sqrt(HDIM)
    group = jnp.arange(TOKENS) // span
    inside = group[:, None] == group[None, :]
    scores = jnp.where(inside, scores, -jnp.inf)
    raised = jnp.exp(scores - jnp.max(scores, axis=-1, keepdims=True))
    prob = raised / jnp.sum(raised, axis=-1, keepdims=True)
    weights = half(prob)
    context = half(mm(weights, values))
    return query, keyset, values, prob, weights, context


def attend_back(saved, gradient, output_weight):
    query, keyset, values, prob, weights, context = saved
    d_context = half(mm_nt(gradient, output_weight))
    d_values = half(mm_tn(weights, d_context))
    d_probs = mm_nt(d_context, values)
    d_scores = half(
        prob * (d_probs - jnp.sum(prob * d_probs, axis=-1, keepdims=True)) / math.sqrt(HDIM)
    )
    d_query = half(mm(d_scores, keyset))
    d_keys = half(mm_tn(d_scores, query))
    return jnp.concatenate((d_query, d_keys, d_values), axis=1)


def weight_terms(left, right):
    return half(SCALE * mm_tn(left, right))


def per_device(
    spatial_input_rows,
    x_temporal,
    cotangent,
    spatial_query_key_value,
    spatial_output_weight,
    temporal_query_key_value,
    temporal_output_weight,
    up_weight,
    down_weight,
):
    width = D // 16
    qkv_t = temporal_query_key_value.reshape(D, 3 * HDIM)
    qkv_s = spatial_query_key_value.reshape(D, 3 * HDIM)

    pair = jnp.stack((x_temporal[:, 0], cotangent[:, 0])).reshape(2, 2, 16, 8, width)
    pair = lax.all_to_all(jnp.transpose(pair, (2, 0, 1, 3, 4)), SEQ, 0, 0, tiled=True)
    pair = jnp.transpose(pair, (2, 1, 3, 0, 4)).reshape(2, 2 * HALF, width)
    pair = features_whole(own_first(pair))
    both_pair = jnp.stack((pair, swap(pair))).reshape(2, 2, HALF, D)
    x_rows = both_pair[:, 0].reshape(TOKENS, D)
    upstream = both_pair[:, 1].reshape(TOKENS, D)

    inverse_t, centered_t = normalize(x_rows)
    normed_t = half(centered_t)
    saved_t = attend(normed_t, qkv_t, FRAMES)
    context_t = saved_t[5]
    attn_own = reduce_rows(context_t, temporal_output_weight.T)
    x_own = own_rows(x_rows)
    inverse_own, centered_own = normalize(x_own)

    middle_own = half(wide(x_own) + attn_own)
    inverse_m, centered_m = normalize(middle_own)
    normed_m = rows_whole(half(centered_m))
    value, slope = gelu_both(mm(normed_m, up_weight))
    hidden = half(value)
    d_pre = half(mm_nt(upstream, down_weight) * slope)
    d_norm_m = reduce_rows(d_pre, up_weight)
    mlp_terms = jnp.concatenate(
        (weight_terms(normed_m, d_pre), weight_terms(upstream, hidden)), axis=1
    )
    mlp_grads = sum_tokens(mlp_terms)
    d_middle_own = normalize_back(own_rows(upstream), inverse_m, centered_m, d_norm_m)
    d_middle = rows_whole(d_middle_own)

    d_qkv_t = attend_back(saved_t, d_middle, temporal_output_weight)
    d_norm_t = reduce_rows(d_qkv_t, qkv_t)
    temporal_terms = jnp.concatenate(
        (weight_terms(normed_t, d_qkv_t), weight_terms(d_middle, context_t)), axis=1
    )
    temporal_grads = sum_tokens(temporal_terms)
    d_temporal_own = normalize_back(d_middle_own, inverse_own, centered_own, d_norm_t)

    d_frame_own = lax.all_to_all(d_temporal_own, SEQ, 0, 0, tiled=True)
    d_frame = rows_whole(d_frame_own)

    rows = jnp.transpose(spatial_input_rows.reshape(2, 16, 8, width), (0, 2, 1, 3))
    s_rows = both(features_whole(own_first(rows.reshape(2, HALF, width))))
    inverse_s, centered_s = normalize(s_rows)
    normed_s = half(centered_s)
    saved_s = attend(normed_s, qkv_s, PATCHES)
    d_qkv_s = attend_back(saved_s, d_frame, spatial_output_weight)
    spatial_terms = jnp.concatenate(
        (weight_terms(normed_s, d_qkv_s), weight_terms(d_frame, saved_s[5])), axis=1
    )
    spatial_grads = sum_tokens(spatial_terms)
    d_norm_s = reduce_rows(d_qkv_s, qkv_s)
    inverse_own_s, centered_own_s = normalize(own_rows(s_rows))
    result_own = normalize_back(d_frame_own, inverse_own_s, centered_own_s, d_norm_s)
    result = jnp.transpose(result_own.reshape(16, 16, width), (1, 0, 2))
    result = lax.all_to_all(result, TP, 0, 0, tiled=True)
    result = jnp.transpose(result.reshape(8, 2, 16, width), (1, 2, 0, 3))

    split = 3 * HDIM
    return (
        result.reshape(2, 1, PATCHES, width),
        spatial_grads[:, :split].reshape(-1, 3, HDIM),
        spatial_grads[:, split:].T,
        temporal_grads[:, :split].reshape(-1, 3, HDIM),
        temporal_grads[:, split:].T,
        mlp_grads[:, :split],
        mlp_grads[:, split:].T,
    )


def solution(mesh):
    fine = Mesh(mesh.devices.reshape(4, 4, 2, 4, 2), SEQ + TP)
    stream = P(None, SEQ, None, TP)
    return jax.shard_map(
        per_device,
        mesh=fine,
        in_specs=(
            stream,
            stream,
            stream,
            P(None, None, TP),
            P(TP, None),
            P(None, None, TP),
            P(TP, None),
            P(None, TP),
            P(TP, None),
        ),
        out_specs=(
            stream,
            P(SEQ, None, TP),
            P(TP, SEQ),
            P(SEQ, None, TP),
            P(TP, SEQ),
            P(SEQ, TP),
            P(TP, SEQ),
        ),
        check_vma=False,
    )
```

time: 1340 us -> 495 us (0.37)
  waiting for transfers between devices: 1160 us -> 195 us
  starting transfers between devices: 0.98 us -> 96.7 us
  blocking collectives: 54.7 us -> 73 us
  other arithmetic: 17.3 us -> 34.4 us
    reduce_scatter x6 -> x0, waiting for transfers between devices: 515 us -> none  [the longest x3 265 us: column_grads(): lax.psum_scatter(term.astype(jnp.bfloat16), 'seq', scatter_dimension=1, t...]
    psum x4 -> x0, waiting for transfers between devices: 487 us -> none  [head_whole(): lax.psum(portion_value.astype(jnp.bfloat16), 'tp').astype(jnp.float32)]
    all_to_all x0 -> x14, waiting for transfers between devices: none -> 182 us  [the longest x3 108 us: sum_tokens(): pieces = lax.all_to_all(term.reshape(4, D // 4, -1), 'y', 0, 0, tiled=True)]
    all_gather x4 -> x0, waiting for transfers between devices: 155 us -> none  [the longest x1 55.2 us: per_device(): lax.all_gather(upper_portion, 'tp', axis=3, tiled=True)]
    all_to_all x0 -> x14, starting transfers between devices: none -> 94.3 us  [the longest x3 24.4 us: sum_tokens(): lax.all_to_all(part.reshape(4, D // 16, -1), 'zh', 0, 0, tiled=True)]
    all_gather x4 -> x0, local copies, waits for them, and re-layouts: 33.2 us -> none  [the longest x1 13 us: per_device(): lax.all_gather(upper_portion, 'tp', axis=3, tiled=True)]
    all_to_all x3 -> x4, blocking collectives: 54.7 us -> 73 us  [the longest x3 56.9 us: spread(): return lax.all_to_all(copies, RING, 0, 0, tiled=True)]
    reduce_sum x6 -> x19, other arithmetic: 8.3 us -> 22.1 us  [the longest x3 10.1 us: sum_tokens(): part = half(jnp.sum(wide(pieces), axis=0))]
  transfers between devices with their start and end apart: 14 -> 25, of which waited for: 14 -> 22; matrix products, arithmetic and copies ran while one was open for 6% -> 17% of each run, Pallas kernels for 0% -> 0%
where the time goes in v1:
time: 495 us; the launch traced here: 491 us
  waiting for transfers between devices  195 us (39%)
  starting transfers between devices  96.7 us (20%)
  blocking collectives  73 us (15%)
  local copies, waits for them, and re-layouts  55.2 us (11%)
  matrix products  35.3 us (7%)
  other arithmetic  34.4 us (7%)
    all_to_all x3, waiting for transfers between devices, sum_tokens(): pieces = lax.all_to_all(term.reshape(4, D // 4, -1), 'y', 0, 0, tiled=True)  108 us
    all_to_all x3, blocking collectives, spread(): return lax.all_to_all(copies, RING, 0, 0, tiled=True)  56.9 us
    dot_general x31, matrix products, dot(): lax.dot_general(left, right, (dims, ((), ())), preferred_element_type=jnp...  35.3 us
    all_to_all x3, waiting for transfers between devices, sum_tokens(): lax.all_to_all(part.reshape(4, D // 16, -1), 'zh', 0, 0, tiled=True)  30.4 us
    all_to_all x3, starting transfers between devices, sum_tokens(): lax.all_to_all(part.reshape(4, D // 16, -1), 'zh', 0, 0, tiled=True)  24.4 us
    all_to_all x3, starting transfers between devices, reduce_rows(): lax.all_to_all(mine.reshape(CHIPS, HALF // CHIPS, D), RING, 0, 0, tiled=T...  23 us
    unnamed x109, local copies, waits for them, and re-layouts  21.4 us
    all_to_all x3, waiting for transfers between devices, reduce_rows(): lax.all_to_all(mine.reshape(CHIPS, HALF // CHIPS, D), RING, 0, 0, tiled=T...  17 us
  transfers between devices with their start and end apart: 25, of which 22 were waited for; matrix products, arithmetic and copies ran while one was open for 17% of the time, Pallas kernels for 0%

profile of v1, /device:TPU:2, one launch (start us, length us, event | category | flops | bytes accessed | tf_op | source)
XLA Modules:
  0.0 491.5 jit_solution(18402144917917082090)
XLA Ops:
  3.6 11.2 %all-to-all-start = ((bf16[16,2,2,8,192]{4,3,2,1,0:T(8,128)(2,1)}), bf16[16,2,2,8,192]{4,3,2,1,0:T(8,128)(2,1)S(1)}, u32[]{:S(2)}, u32[]{:S(2)}) async-start(bf16[16,2,2,8,192]{4,3,2,1,0:T(8,128)(2,1)} %copy.83), calls=%async_computation | async-start | bytes 524288 | tf_op jit(solution)/shard_map/all_to_all | solution.py:169
  14.8 13.3 %all-to-all-done = bf16[16,2,2,8,192]{4,3,2,1,0:T(8,128)(2,1)S(1)} async-done(((bf16[16,2,2,8,192]{4,3,2,1,0:T(8,128)(2,1)}), bf16[16,2,2,8,192]{4,3,2,1,0:T(8,128)(2,1)S(1)}, u32[]{:S(2)}, u32[]{:S(2)}) %all-to-all-start) | async-done | bytes 196640 | tf_op jit(solution)/shard_map/all_to_all | solution.py:169
  30.1 25.0 %all_to_all.94 = bf16[8,256,384]{1,2,0:T(8,128)(2,1)} all-to-all(bf16[8,256,384]{1,2,0:T(8,128)(2,1)S(1)} %broadcast_in_dim.15), channel_id=1, replica_groups=mesh['y'=4,'zh'=4,'zl'=2,'x'=4,'c'=2] {'zl','x'}, dimensions={0} | all-to-all | bytes 3145728 | tf_op jit(solution)/shard_map/all_to_all | solution.py:76
  55.1 4.3 copy.88
  59.4 3.5 reshape.541
  63.0 4.9 %copy.108 = bf16[1,2,128,3072]{3,2,1,0:T(8,128)(2,1)} copy(bf16[1,2,128,3072]{2,1,3,0:T(2,128)(2,1)} %reshape.541) | data formatting | bytes 3145728 | tf_op jit(solution)/shard_map/stack | solution.py:172
  80.9 5.9 %all-to-all-start.2 = ((bf16[8,16,3072]{2,1,0:T(8,128)(2,1)}), bf16[8,16,3072]{2,1,0:T(8,128)(2,1)}, u32[]{:S(2)}, u32[]{:S(2)}) async-start(bf16[8,16,3072]{2,1,0:T(8,128)(2,1)} %bitcast.216), calls=%async_computation.2 | async-start | bytes 1572864 | tf_op jit(solution)/shard_map/all_to_all | solution.py:105
  89.5 9.1 %all-to-all-done.2 = bf16[8,16,3072]{2,1,0:T(8,128)(2,1)} async-done(((bf16[8,16,3072]{2,1,0:T(8,128)(2,1)}), bf16[8,16,3072]{2,1,0:T(8,128)(2,1)}, u32[]{:S(2)}, u32[]{:S(2)}) %all-to-all-start.2) | async-done | bytes 786464 | tf_op jit(solution)/shard_map/all_to_all | solution.py:105
  101.7 15.9 %all_to_all.95 = bf16[8,16,3072]{2,1,0:T(8,128)(2,1)S(1)} all-to-all(bf16[8,16,3072]{2,1,0:T(8,128)(2,1)S(1)} %broadcast_in_dim.17), channel_id=1, replica_groups=mesh['y'=4,'zh'=4,'zl'=2,'x'=4,'c'=2] {'zl','x'}, dimensions={0} | all-to-all | bytes 1572864 | tf_op jit(solution)/shard_map/all_to_all | solution.py:76
  127.6 16.1 %all_to_all.96 = bf16[8,16,3072]{2,1,0:T(8,128)(2,1)S(1)} all-to-all(bf16[8,16,3072]{2,1,0:T(8,128)(2,1)S(1)} %bitcast.218), channel_id=1, replica_groups=mesh['y'=4,'zh'=4,'zl'=2,'x'=4,'c'=2] {'zl','x'}, dimensions={0} | all-to-all | bytes 1572864 | tf_op jit(solution)/shard_map/all_to_all | solution.py:105
  145.6 16.0 %all_to_all.97 = bf16[8,16,3072]{2,1,0:T(8,128)(2,1)S(1)} all-to-all(bf16[8,16,3072]{2,1,0:T(8,128)(2,1)S(1)} %broadcast_in_dim.18), channel_id=1, replica_groups=mesh['y'=4,'zh'=4,'zl'=2,'x'=4,'c'=2] {'zl','x'}, dimensions={0} | all-to-all | bytes 1572864 | tf_op jit(solution)/shard_map/all_to_all | solution.py:76
  174.0 5.3 %all-to-all-start.6 = ((bf16[8,16,3072]{2,1,0:T(8,128)(2,1)}), bf16[8,16,3072]{2,1,0:T(8,128)(2,1)S(1)}, u32[]{:S(2)}, u32[]{:S(2)}) async-start(bf16[8,16,3072]{2,1,0:T(8,128)(2,1)} %bitcast.23), calls=%async_computation.6 | async-start | bytes 1572864 | tf_op jit(solution)/shard_map/all_to_all | solution.py:105
  180.9 3.8 multiply_convert_fusion
  184.6 6.1 %all-to-all-done.6 = bf16[8,16,3072]{2,1,0:T(8,128)(2,1)S(1)} async-done(((bf16[8,16,3072]{2,1,0:T(8,128)(2,1)}), bf16[8,16,3072]{2,1,0:T(8,128)(2,1)S(1)}, u32[]{:S(2)}, u32[]{:S(2)}) %all-to-all-start.6) | async-done | bytes 786464 | tf_op jit(solution)/shard_map/all_to_all | solution.py:105
  191.8 4.8 all-to-all-start.8
  216.3 5.5 %all-to-all-done.7 = bf16[16,2,1536]{2,1,0:T(2,128)(2,1)S(1)} async-done(((bf16[16,2,1536]{2,1,0:T(2,128)(2,1)}), bf16[16,2,1536]{2,1,0:T(2,128)(2,1)S(1)}, u32[]{:S(2)}, u32[]{:S(2)}) %all-to-all-start.7) | async-done | bytes 98336 | tf_op jit(solution)/shard_map/all_to_all | solution.py:206
  221.8 4.9 %all-to-all-start.16 = ((bf16[4,768,768]{1,2,0:T(8,128)(2,1)}), bf16[4,768,768]{1,2,0:T(8,128)(2,1)}, u32[]{:S(2)}, u32[]{:S(2)}) async-start(bf16[4,768,768]{1,2,0:T(8,128)(2,1)} %bitcast.199), calls=%async_computation.16 | async-start | bytes 9437184 | tf_op jit(solution)/shard_map/all_to_all | solution.py:110
  226.9 52.5 %all-to-all-done.16 = bf16[4,768,768]{1,2,0:T(8,128)(2,1)} async-done(((bf16[4,768,768]{1,2,0:T(8,128)(2,1)}), bf16[4,768,768]{1,2,0:T(8,128)(2,1)}, u32[]{:S(2)}, u32[]{:S(2)}) %all-to-all-start.16) | async-done | bytes 4718624 | tf_op jit(solution)/shard_map/all_to_all | solution.py:110
  280.4 6.2 %all-to-all-start.9 = ((bf16[8,16,3072]{2,1,0:T(8,128)(2,1)}), bf16[8,16,3072]{2,1,0:T(8,128)(2,1)S(1)}, u32[]{:S(2)}, u32[]{:S(2)}) async-start(bf16[8,16,3072]{2,1,0:T(8,128)(2,1)} %broadcast_in_dim.20), calls=%async_computation.9 | async-start | bytes 1572864 | tf_op jit(solution)/shard_map/all_to_all | solution.py:76
  297.0 4.7 all-to-all-start.14
  309.9 3.8 reduce_sum.245
  315.1 22.9 %all-to-all-done.14 = bf16[4,768,512]{1,2,0:T(8,128)(2,1)} async-done(((bf16[4,768,512]{1,2,0:T(8,128)(2,1)}), bf16[4,768,512]{1,2,0:T(8,128)(2,1)}, u32[]{:S(2)}, u32[]{:S(2)}) %all-to-all-start.14) | async-done | bytes 3145760 | tf_op jit(solution)/shard_map/all_to_all | solution.py:110
  338.0 3.5 all-to-all-start.17
  354.3 7.7 %all-to-all-done.17 = bf16[4,192,768]{2,1,0:T(8,128)(2,1)S(1)} async-done(((bf16[4,192,768]{2,1,0:T(8,128)(2,1)}), bf16[4,192,768]{2,1,0:T(8,128)(2,1)S(1)}, u32[]{:S(2)}, u32[]{:S(2)}) %all-to-all-start.17) | async-done | bytes 1179680 | tf_op jit(solution)/shard_map/all_to_all | solution.py:112
  362.1 11.2 %all-to-all-start.15 = ((bf16[4,192,512]{2,1,0:T(8,128)(2,1)}), bf16[4,192,512]{2,1,0:T(8,128)(2,1)}, u32[]{:S(2)}, u32[]{:S(2)}) async-start(bf16[4,192,512]{2,1,0:T(8,128)(2,1)} %bitcast.214), calls=%async_computation.15 | async-start | bytes 1572864 | tf_op jit(solution)/shard_map/all_to_all | solution.py:112
  378.7 8.7 %all-to-all-done.15 = bf16[4,192,512]{2,1,0:T(8,128)(2,1)} async-done(((bf16[4,192,512]{2,1,0:T(8,128)(2,1)}), bf16[4,192,512]{2,1,0:T(8,128)(2,1)}, u32[]{:S(2)}, u32[]{:S(2)}) %all-to-all-start.15) | async-done | bytes 786464 | tf_op jit(solution)/shard_map/all_to_all | solution.py:112
  387.4 11.8 %all-to-all-start.10 = ((bf16[8,16,3072]{2,1,0:T(8,128)(2,1)}), bf16[8,16,3072]{2,1,0:T(8,128)(2,1)S(1)}, u32[]{:S(2)}, u32[]{:S(2)}) async-start(bf16[8,16,3072]{2,1,0:T(8,128)(2,1)} %bitcast.217), calls=%async_computation.10 | async-start | bytes 1572864 | tf_op jit(solution)/shard_map/all_to_all | solution.py:105
  407.4 4.8 all-to-all-start.12
  413.7 32.6 %all-to-all-done.12 = bf16[4,768,512]{1,2,0:T(8,128)(2,1)} async-done(((bf16[4,768,512]{1,2,0:T(8,128)(2,1)}), bf16[4,768,512]{1,2,0:T(8,128)(2,1)}, u32[]{:S(2)}, u32[]{:S(2)}) %all-to-all-start.12) | async-done | bytes 3145760 | tf_op jit(solution)/shard_map/all_to_all | solution.py:110
  446.3 6.8 %all-to-all-start.11 = ((bf16[16,16,192]{2,1,0:T(8,128)(2,1)}), bf16[16,16,192]{2,1,0:T(8,128)(2,1)}, u32[]{:S(2)}, u32[]{:S(2)}) async-start(bf16[16,16,192]{2,1,0:T(8,128)(2,1)} %copy.94), calls=%async_computation.11 | async-start | bytes 262144 | tf_op jit(solution)/shard_map/all_to_all | solution.py:223
  458.2 9.7 %all-to-all-start.13 = ((bf16[4,192,512]{2,1,0:T(8,128)(2,1)}), bf16[4,192,512]{2,1,0:T(8,128)(2,1)}, u32[]{:S(2)}, u32[]{:S(2)}) async-start(bf16[4,192,512]{2,1,0:T(8,128)(2,1)} %bitcast.215), calls=%async_computation.13 | async-start | bytes 1572864 | tf_op jit(solution)/shard_map/all_to_all | solution.py:112
  474.8 14.1 %all-to-all-done.13 = bf16[4,192,512]{2,1,0:T(8,128)(2,1)} async-done(((bf16[4,192,512]{2,1,0:T(8,128)(2,1)}), bf16[4,192,512]{2,1,0:T(8,128)(2,1)}, u32[]{:S(2)}, u32[]{:S(2)}) %all-to-all-start.13) | async-done | bytes 786464 | tf_op jit(solution)/shard_map/all_to_all | solution.py:112
  (242 shorter events, 133.4 us)
Async XLA Ops:
  0.6 119.3 %copy-start = (bf16[3072,384]{1,0:T(8,128)(2,1)S(1)}, bf16[3072,384]{1,0:T(8,128)(2,1)}, u32[]{:S(2)}) copy-start(bf16[3072,384]{1,0:T(8,128)(2,1)} %param.16) | copy-start | bytes 7077892
  3.6 24.5 %all-to-all-start = ((bf16[16,2,2,8,192]{4,3,2,1,0:T(8,128)(2,1)}), bf16[16,2,2,8,192]{4,3,2,1,0:T(8,128)(2,1)S(1)}, u32[]{:S(2)}, u32[]{:S(2)}) async-start(bf16[16,2,2,8,192]{4,3,2,1,0:T(8,128)(2,1)} %copy.83), calls=%async_computation | async-start | bytes 524288 | tf_op jit(solution)/shard_map/all_to_all | solution.py:169
  28.3 1.4 collective-permute-start
  55.1 12.8 %collective-permute-start.1 = (bf16[256,3072]{0,1:T(8,128)(2,1)}, bf16[256,3072]{0,1:T(8,128)(2,1)}, u32[]{:S(2)}, u32[]{:S(2)}) collective-permute-start(bf16[256,3072]{0,1:T(8,128)(2,1)} %bitcast.10), channel_id=1, source_target_pairs={{0,1},{1,0},{2,3},{3,2},{4,5},{5,4},{6,7},{7,6},{8,9},{9,8},{10,11... | collective-permute-start | bytes 4718600 | tf_op jit(solution)/shard_map/ppermute | solution.py:71
  77.1 2.5 collective-permute-start.2
  80.9 17.7 %all-to-all-start.2 = ((bf16[8,16,3072]{2,1,0:T(8,128)(2,1)}), bf16[8,16,3072]{2,1,0:T(8,128)(2,1)}, u32[]{:S(2)}, u32[]{:S(2)}) async-start(bf16[8,16,3072]{2,1,0:T(8,128)(2,1)} %bitcast.216), calls=%async_computation.2 | async-start | bytes 1572864 | tf_op jit(solution)/shard_map/all_to_all | solution.py:105
  98.6 19.0 %copy-start.3 = (bf16[1,2,128,3072]{3,2,1,0:T(8,128)(2,1)S(1)}, bf16[1,2,128,3072]{3,2,1,0:T(8,128)(2,1)}, u32[]{:S(2)}) copy-start(bf16[1,2,128,3072]{3,2,1,0:T(8,128)(2,1)} %copy.108) | copy-start | bytes 4718596
  98.6 19.0 %copy-start.5 = (bf16[256,3072]{1,0:T(8,128)(2,1)S(1)}, bf16[256,3072]{1,0:T(8,128)(2,1)}, u32[]{:S(2)}) copy-start(bf16[256,3072]{1,0:T(8,128)(2,1)} %copy.87) | copy-start | bytes 4718596
  117.6 2.3 collective-permute-start.3
  124.2 2.5 collective-permute-start.4
  145.6 19.9 %copy-start.15 = (f32[256,256]{0,1:T(8,128)S(1)}, f32[256,256]{0,1:T(8,128)}, u32[]{:S(2)}) copy-start(f32[256,256]{0,1:T(8,128)} %copy-done.14) | copy-start | bytes 786436
  161.7 2.3 collective-permute-start.5
  168.7 2.7 collective-permute-start.6
  174.0 16.7 %all-to-all-start.6 = ((bf16[8,16,3072]{2,1,0:T(8,128)(2,1)}), bf16[8,16,3072]{2,1,0:T(8,128)(2,1)S(1)}, u32[]{:S(2)}, u32[]{:S(2)}) async-start(bf16[8,16,3072]{2,1,0:T(8,128)(2,1)} %bitcast.23), calls=%async_computation.6 | async-start | bytes 1572864 | tf_op jit(solution)/shard_map/all_to_all | solution.py:105
  179.4 1.3 collective-permute-start.7
  184.6 11.9 %copy-start.31 = (bf16[256,384]{1,0:T(8,128)(2,1)S(1)}, bf16[256,384]{1,0:T(8,128)(2,1)}, u32[]{:S(2)}) copy-start(bf16[256,384]{1,0:T(8,128)(2,1)} %copy-done.30) | copy-start | bytes 589828
  191.8 15.8 %all-to-all-start.8 = ((bf16[8,128,384]{2,1,0:T(8,128)(2,1)}), bf16[8,128,384]{2,1,0:T(8,128)(2,1)S(1)}, u32[]{:S(2)}, u32[]{:S(2)}) async-start(bf16[8,128,384]{2,1,0:T(8,128)(2,1)} %broadcast_in_dim.19), calls=%async_computation.8 | async-start | bytes 1572864 | tf_op jit(solution)/shard_map/all_to_all | solution.py:76
  207.6 14.2 %all-to-all-start.7 = ((bf16[16,2,1536]{2,1,0:T(2,128)(2,1)}), bf16[16,2,1536]{2,1,0:T(2,128)(2,1)S(1)}, u32[]{:S(2)}, u32[]{:S(2)}) async-start(bf16[16,2,1536]{2,1,0:T(2,128)(2,1)} %reshape.542), calls=%async_computation.7 | async-start | bytes 196608 | tf_op jit(solution)/shard_map/all_to_all | solution.py:206
  221.8 57.6 %all-to-all-start.16 = ((bf16[4,768,768]{1,2,0:T(8,128)(2,1)}), bf16[4,768,768]{1,2,0:T(8,128)(2,1)}, u32[]{:S(2)}, u32[]{:S(2)}) async-start(bf16[4,768,768]{1,2,0:T(8,128)(2,1)} %bitcast.199), calls=%async_computation.16 | async-start | bytes 9437184 | tf_op jit(solution)/shard_map/all_to_all | solution.py:110
  226.8 62.1 %copy-start.11 = (bf16[16,1,3072]{2,1,0:T(2,128)(2,1)}, bf16[16,1,3072]{2,1,0:T(2,128)(2,1)S(1)}, u32[]{:S(2)}) copy-start(bf16[16,1,3072]{2,1,0:T(2,128)(2,1)S(1)} %reshape.543) | copy-start | bytes 294916
  280.4 15.6 %all-to-all-start.9 = ((bf16[8,16,3072]{2,1,0:T(8,128)(2,1)}), bf16[8,16,3072]{2,1,0:T(8,128)(2,1)S(1)}, u32[]{:S(2)}, u32[]{:S(2)}) async-start(bf16[8,16,3072]{2,1,0:T(8,128)(2,1)} %broadcast_in_dim.20), calls=%async_computation.9 | async-start | bytes 1572864 | tf_op jit(solution)/shard_map/all_to_all | solution.py:76
  297.0 41.1 %all-to-all-start.14 = ((bf16[4,768,512]{1,2,0:T(8,128)(2,1)}), bf16[4,768,512]{1,2,0:T(8,128)(2,1)}, u32[]{:S(2)}, u32[]{:S(2)}) async-start(bf16[4,768,512]{1,2,0:T(8,128)(2,1)} %bitcast.201), calls=%async_computation.14 | async-start | bytes 6291456 | tf_op jit(solution)/shard_map/all_to_all | solution.py:110
  301.8 3.1 collective-permute-start.8
  306.4 42.9 %collective-permute-start.9 = (bf16[128,3072]{1,0:T(8,128)(2,1)}, bf16[128,3072]{1,0:T(8,128)(2,1)}, u32[]{:S(2)}, u32[]{:S(2)}) collective-permute-start(bf16[128,3072]{1,0:T(8,128)(2,1)} %bitcast.227), channel_id=1, source_target_pairs={{0,1},{1,0},{2,3},{3,2},{4,5},{5,4},{6,7},{7,6},{8,9},{9,8},{10,11... | collective-permute-start | bytes 2359304 | tf_op jit(solution)/shard_map/ppermute | solution.py:71
  338.0 24.0 %all-to-all-start.17 = ((bf16[4,192,768]{2,1,0:T(8,128)(2,1)}), bf16[4,192,768]{2,1,0:T(8,128)(2,1)S(1)}, u32[]{:S(2)}, u32[]{:S(2)}) async-start(bf16[4,192,768]{2,1,0:T(8,128)(2,1)} %bitcast.205), calls=%async_computation.17 | async-start | bytes 2359296 | tf_op jit(solution)/shard_map/all_to_all | solution.py:112
  362.1 25.3 %all-to-all-start.15 = ((bf16[4,192,512]{2,1,0:T(8,128)(2,1)}), bf16[4,192,512]{2,1,0:T(8,128)(2,1)}, u32[]{:S(2)}, u32[]{:S(2)}) async-start(bf16[4,192,512]{2,1,0:T(8,128)(2,1)} %bitcast.214), calls=%async_computation.15 | async-start | bytes 1572864 | tf_op jit(solution)/shard_map/all_to_all | solution.py:112
  374.9 2.4 collective-permute-start.10
  387.4 20.0 %all-to-all-start.10 = ((bf16[8,16,3072]{2,1,0:T(8,128)(2,1)}), bf16[8,16,3072]{2,1,0:T(8,128)(2,1)S(1)}, u32[]{:S(2)}, u32[]{:S(2)}) async-start(bf16[8,16,3072]{2,1,0:T(8,128)(2,1)} %bitcast.217), calls=%async_computation.10 | async-start | bytes 1572864 | tf_op jit(solution)/shard_map/all_to_all | solution.py:105
  407.4 38.9 %all-to-all-start.12 = ((bf16[4,768,512]{1,2,0:T(8,128)(2,1)}), bf16[4,768,512]{1,2,0:T(8,128)(2,1)}, u32[]{:S(2)}, u32[]{:S(2)}) async-start(bf16[4,768,512]{1,2,0:T(8,128)(2,1)} %bitcast.202), calls=%async_computation.12 | async-start | bytes 6291456 | tf_op jit(solution)/shard_map/all_to_all | solution.py:110
  446.3 11.8 %all-to-all-start.11 = ((bf16[16,16,192]{2,1,0:T(8,128)(2,1)}), bf16[16,16,192]{2,1,0:T(8,128)(2,1)}, u32[]{:S(2)}, u32[]{:S(2)}) async-start(bf16[16,16,192]{2,1,0:T(8,128)(2,1)} %copy.94), calls=%async_computation.11 | async-start | bytes 262144 | tf_op jit(solution)/shard_map/all_to_all | solution.py:223
  458.2 30.7 %all-to-all-start.13 = ((bf16[4,192,512]{2,1,0:T(8,128)(2,1)}), bf16[4,192,512]{2,1,0:T(8,128)(2,1)}, u32[]{:S(2)}, u32[]{:S(2)}) async-start(bf16[4,192,512]{2,1,0:T(8,128)(2,1)} %bitcast.215), calls=%async_computation.13 | async-start | bytes 1572864 | tf_op jit(solution)/shard_map/all_to_all | solution.py:112
  467.8 23.7 %copy-start.1 = (bf16[3072,384]{1,0:T(8,128)(2,1)S(1)}, bf16[3072,384]{1,0:T(8,128)(2,1)}, u32[]{:S(2)}) copy-start(bf16[3072,384]{1,0:T(8,128)(2,1)} %param.16) | copy-start | bytes 7077892
  (42 other events, 115.2 us)
